TPU v7x, 32 devices: a whole 2x2x4 slice. The times are simulated.
32 devices in a mesh: chain: 2 (over y), gx: 16 (over z, x, core).
Axes of the slice: x: 2, y: 2, z: 4, core: 2. Of those that a mesh axis runs over, the one named last changes fastest.
Arguments:
- courant: float32 [32, 128, 4, 128], P(('chain', 'gx')), parts along dimension 0, may hold values from 0.05 to 0.18
- ckpt_prev: float32 [32, 128, 4, 128], P(('chain', 'gx')), parts along dimension 0, may hold values from -6 to 6
- ckpt_cur: float32 [32, 128, 4, 128], P(('chain', 'gx')), parts along dimension 0, may hold values from -6 to 6
- adj_next: float32 [32, 128, 4, 128], P(('chain', 'gx')), parts along dimension 0, may hold values from -6 to 6
- adj_cur: float32 [32, 128, 4, 128], P(('chain', 'gx')), parts along dimension 0, may hold values from -6 to 6
- rec_x: int32 [4096], P(('chain', 'gx')), parts along dimension 0, may hold values from 0 to 255
- rec_plane: int32 [4096], P(('chain', 'gx')), parts along dimension 0, may hold values from 0 to 4095
- traces: float32 [4, 4096], P(None, ('chain', 'gx')), parts along dimension 1, may hold values from -6 to 6
- mass_kernel: float32 [256, 1024], P(None, 'gx'), may hold values from 0.003 to 0.03
Outputs:
- mass_gradient: float32 [32, 128, 4, 128], P(('chain', 'gx')), parts along dimension 0
- adjoint_first: float32 [32, 128, 4, 128], P(('chain', 'gx')), parts along dimension 0
- adjoint_second: float32 [32, 128, 4, 128], P(('chain', 'gx')), parts along dimension 0
There are 2 independent parts, one for each index of `chain`. A program takes and returns all parts, laid end to end along the dimension named above; an argument that names none is the same for every part. Nothing has to cross between parts.
Inputs may be any that keep to these rules, and one draw needn't show every extreme that they name: `rec_x`: several receivers may share a cell; some x ranges hold many more receivers than others.
All inputs are finite; a program needn't handle non-finite values.
Results may differ from a plain program's by a relative error of at most 0.00007.
Values sent between devices are 32-bit elements; how exact they have to be, the bound alone decides.
A program may use at most 64 MiB of HBM per device.

v0:
```python
import functools
import math

import jax
import jax.numpy as jnp
import numpy as np
from jax import lax
from jax.experimental import pallas as pl
from jax.experimental.pallas import tpu as pltpu
from jax.sharding import PartitionSpec as P

GY = 8
STEPS = 4


STENCIL_COEF = (-205.0 / 72.0, 8.0 / 5.0, -1.0 / 5.0, 8.0 / 315.0, -1.0 / 560.0)


MESH = pl.DeviceIdType.MESH
HIGHEST = lax.Precision.HIGHEST


def dot_f32(left, right, left_dim=1, right_dim=0):
    return lax.dot_general(
        left,
        right,
        (((left_dim,), (right_dim,)), ((), ())),
        precision=HIGHEST,
        preferred_element_type=jnp.float32,
    )


def stencil_tables(z_depth, y_cols, chunk):
    coef = np.array(STENCIL_COEF, np.float64)
    halo = 4 * z_depth
    row = np.arange(chunk)[:, None]
    col = np.arange(chunk + 2 * halo)[None, :] - halo
    dx = np.abs(row // z_depth - col // z_depth)
    dz = np.abs(row % z_depth - col % z_depth)
    band = np.where((dz == 0) & (dx <= 4), coef[np.minimum(dx, 4)], 0.0)
    band = band + np.where((dx == 0) & (dz <= 4), coef[np.minimum(dz, 4)], 0.0)
    lane = np.arange(y_cols)
    dy = np.abs(lane[:, None] - lane[None, :])
    along_y = np.where(dy <= 4, coef[np.minimum(dy, 4)], 0.0)
    along_y = np.kron(np.eye(2), along_y)
    edge = np.arange(halo)
    near = edge[:, None] // z_depth + 4 - edge[None, :] // z_depth
    same = edge[:, None] % z_depth == edge[None, :] % z_depth
    from_low = np.where(same & (near <= 4), coef[np.minimum(near, 4)], 0.0)
    far = 4 + edge[None, :] // z_depth - edge[:, None] // z_depth
    from_high = np.where(same & (far <= 4), coef[np.minimum(far, 4)], 0.0)
    rim = np.zeros((16, 2 * y_cols))
    for field in range(2):
        for depth in range(4):
            for y in range(4):
                if y + 4 - depth <= 4:
                    rim[field * 4 + depth, field * y_cols + y] = coef[y + 4 - depth]
                last = y_cols - 1 - y
                gap = y_cols + depth - last
                if gap <= 4:
                    rim[8 + field * 4 + depth, field * y_cols + last] = coef[gap]
    pick = np.zeros((16, 2 * y_cols))
    for field in range(2):
        for depth in range(4):
            pick[field * 4 + depth, field * y_cols + depth] = 1.0
            pick[8 + field * 4 + depth, field * y_cols + y_cols - 4 + depth] = 1.0
    tables = (band, along_y, from_low, from_high, rim, pick)
    return [jnp.asarray(table.astype(np.float32)) for table in tables]


def plane_and_part(tile, planes):
    share = GY // planes
    column = lax.rem(tile, GY)
    return column // share, tile // GY * share + lax.rem(column, share)


def plane_holder(plane, part, planes):
    share = GY // planes
    return part // share * GY + plane * share + lax.rem(part, share)


def window_kernel(
    chunk, move_mass,
    model_ref, prev_ref, cur_ref, next_ref, now_ref, rec_ref, mass_ref,
    band_ref, along_ref, low_ref, high_ref, rim_ref, pick_ref,
    grad_ref, first_ref, second_ref, mass_out,
    both, lap, images, waves, adjoints, records, hot, weights, inject,
    x_out, x_in, y_out, y_in, halo_send, halo_recv, rec_send, rec_recv, own_sem,
    mass_in, mass_send, mass_recv, mass_own,
):
    chain = lax.axis_index("chain")
    tile = lax.axis_index("gx")
    devices = lax.axis_size("gx")
    x_blocks = devices // GY
    rows, y_cols = model_ref.shape
    halo = x_out.shape[2]
    column = lax.rem(tile, GY)
    block = tile // GY
    neighbours = (
        lax.rem(block + x_blocks - 1, x_blocks) * GY + column,
        lax.rem(block + 1, x_blocks) * GY + column,
        block * GY + lax.rem(column + GY - 1, GY),
        block * GY + lax.rem(column + 1, GY),
    )
    has_low = (block > 0).astype(jnp.float32)
    has_high = (block < x_blocks - 1).astype(jnp.float32)
    has_left = (column > 0).astype(jnp.float32)
    has_right = (column < GY - 1).astype(jnp.float32)

    own = pltpu.make_async_copy(rec_ref, records.at[0], own_sem)
    own.start()
    barrier = pltpu.get_barrier_semaphore()

    @pl.loop(1, devices)
    def _(step):
        pl.semaphore_signal(
            barrier, inc=1, device_id=(chain, lax.rem(tile + step, devices)), device_id_type=MESH
        )

    both[0:halo, :] = jnp.zeros((halo, 2 * y_cols), jnp.float32)
    both[halo + rows :, :] = jnp.zeros((halo, 2 * y_cols), jnp.float32)
    low_rows = lax.broadcasted_iota(jnp.int32, rim_ref.shape, 0) < 8
    rim = rim_ref[...] * jnp.where(low_rows, has_left, has_right)

    def pack(phase, wave, adjoint):
        both[halo : halo + rows, 0:y_cols] = wave
        both[halo : halo + rows, y_cols:] = model_ref[...] * adjoint
        x_out[phase, 0] = both[halo : 2 * halo, :]
        x_out[phase, 1] = both[rows : halo + rows, :]
        strips = dot_f32(pick_ref[...], both[halo : halo + rows, :], 1, 1)
        y_out[phase, 0] = strips[0:8]
        y_out[phase, 1] = strips[8:16]

    def halo_copies(phase):
        copies = []
        for way in range(4):
            source = x_out if way < 2 else y_out
            target = x_in if way < 2 else y_in
            copies.append(
                pltpu.make_async_remote_copy(
                    src_ref=source.at[phase, way % 2],
                    dst_ref=target.at[phase, 1 - way % 2],
                    send_sem=halo_send.at[phase, way],
                    recv_sem=halo_recv.at[phase, way],
                    device_id=(chain, neighbours[way]),
                    device_id_type=MESH,
                )
            )
        return copies

    def record_copy(step):
        return pltpu.make_async_remote_copy(
            src_ref=rec_ref,
            dst_ref=records.at[step],
            send_sem=rec_send.at[step],
            recv_sem=rec_recv.at[step],
            device_id=(chain, lax.rem(tile + step, devices)),
            device_id_type=MESH,
        )

    slots = mass_in.shape[0]
    _, quarter = plane_and_part(tile, slots)

    def mass_copies(number):
        target = plane_holder(number, tile // slots, slots)
        remote = pltpu.make_async_remote_copy(
            src_ref=mass_ref,
            dst_ref=mass_in.at[lax.rem(tile, slots)],
            send_sem=mass_send.at[number],
            recv_sem=mass_recv.at[lax.rem(tile, slots)],
            device_id=(chain, target),
            device_id_type=MESH,
        )
        local = pltpu.make_async_copy(mass_ref, mass_in.at[lax.rem(tile, slots)], mass_own)
        return target != tile, remote, local

    def mass_start():
        for number in range(slots):
            away, remote, local = mass_copies(number)
            pl.when(away)(remote.start)
            pl.when(jnp.logical_not(away))(local.start)

    def mass_finish():
        for number in range(slots):
            away, remote, local = mass_copies(number)
            pl.when(away)(remote.wait_send)
            pl.when(jnp.logical_not(away))(local.wait)
        for slot in range(slots):
            arrival = pltpu.make_async_remote_copy(
                src_ref=mass_ref,
                dst_ref=mass_in.at[slot],
                send_sem=mass_send.at[slot],
                recv_sem=mass_recv.at[slot],
                device_id=(chain, lax.rem(tile + 1, devices)),
                device_id_type=MESH,
            )
            pl.when(quarter * slots + slot != tile)(arrival.wait_recv)
        mass_out[...] = mass_in[...]

    pack(0, cur_ref[...], now_ref[...])
    pl.semaphore_wait(barrier, devices - 1)
    pending = []
    width = rec_ref.shape[1]
    total = devices * width
    part = math.gcd(total, 2048)
    for phase in range(STEPS):
        copies = halo_copies(phase)
        for copy in copies:
            copy.start()
        pending += copies
        if phase == 0:

            @pl.loop(1, devices)
            def _(step):
                record_copy(step).start()

            if move_mass:
                mass_start()

        lap[...] = dot_f32(both[halo : halo + rows, :], along_ref[...])
        for start in range(0, rows, chunk):
            lap[start : start + chunk, :] += dot_f32(
                band_ref[...], both[start : start + chunk + 2 * halo, :]
            )
        if phase == 0:
            own.wait()

            @pl.loop(1, devices)
            def _(step):
                record_copy(step).wait()

            @pl.loop(0, devices)
            def _(step):
                lanes = pl.ds(pl.multiple_of(step * width, width), width)
                cell = records[step, 0:1, :] - (tile * rows).astype(jnp.float32)
                index = lax.broadcasted_iota(jnp.int32, (rows, width), 0).astype(jnp.float32)
                hot[:, lanes] = jnp.where(index == cell, 1.0, 0.0).astype(jnp.bfloat16)

        section = STEPS - 1 - phase

        @pl.loop(0, devices)
        def _(step):
            lanes = pl.ds(pl.multiple_of(step * width, width), width)
            place = records[step, 1:2, :]
            value = records[step, 2 + section : 3 + section, :]
            index = lax.broadcasted_iota(jnp.int32, (y_cols, width), 0).astype(jnp.float32)
            rest = jnp.where(index == place, value, 0.0)
            for level in range(3):
                piece = rest.astype(jnp.bfloat16)
                weights[level * y_cols : (level + 1) * y_cols, lanes] = piece
                rest = rest - piece.astype(jnp.float32)

        def injected(lanes):
            triple = lax.dot_general(
                hot[:, lanes],
                weights[:, lanes],
                (((1,), (1,)), ((), ())),
                preferred_element_type=jnp.float32,
            )
            return (
                triple[:, 0:y_cols]
                + triple[:, y_cols : 2 * y_cols]
                + triple[:, 2 * y_cols :]
            )

        inject[...] = injected(pl.ds(0, part))
        if total > part:

            @pl.loop(1, total // part)
            def _(step):
                inject[...] += injected(pl.ds(pl.multiple_of(step * part, part), part))

        for copy in copies:
            copy.wait_recv()
        sides = jnp.concatenate((y_in[phase, 0], y_in[phase, 1]), axis=0)
        lap[...] += dot_f32(sides, rim, 0, 0)
        lap[0:halo, :] += has_low * dot_f32(low_ref[...], x_in[phase, 0])
        lap[rows - halo :, :] += has_high * dot_f32(high_ref[...], x_in[phase, 1])
        image = lap[:, 0:y_cols]
        images[phase] = image
        if phase + 1 < STEPS:
            older = prev_ref[...] if phase == 0 else (cur_ref[...] if phase == 1 else waves[0])
            newer = cur_ref[...] if phase == 0 else waves[phase - 1]
            waves[phase] = 2.0 * newer - older + model_ref[...] * image
        later = next_ref[...] if phase == 0 else (now_ref[...] if phase == 1 else adjoints[phase - 2])
        now = now_ref[...] if phase == 0 else adjoints[phase - 1]
        adjoints[phase] = 2.0 * now - later + lap[:, y_cols:] + inject[...]
        if phase + 1 < STEPS:
            pack(phase + 1, waves[phase], adjoints[phase])
    grad_ref[...] = (
        now_ref[...] * images[3]
        + adjoints[0] * images[2]
        + adjoints[1] * images[1]
        + adjoints[2] * images[0]
    )
    first_ref[...] = adjoints[3]
    second_ref[...] = adjoints[2]
    for copy in pending:
        copy.wait_send()
    if move_mass:
        mass_finish()
    else:
        mass_out[...] = jnp.zeros(mass_out.shape, jnp.float32)


def run_window(model, u_prev, u_cur, a_next, a_cur, records, mass, move_mass):
    rows, y_cols = model.shape
    z_depth = 4
    devices = lax.axis_size("gx")
    halo = 4 * z_depth
    chunk = 128
    total = devices * records.shape[1]
    tables = stencil_tables(z_depth, y_cols, chunk)
    field = jax.ShapeDtypeStruct((rows, y_cols), jnp.float32)
    slots = jax.ShapeDtypeStruct((z_depth,) + mass.shape, jnp.float32)
    vmem = pl.BlockSpec(memory_space=pltpu.VMEM)
    return pl.pallas_call(
        functools.partial(window_kernel, chunk, move_mass),
        out_shape=(field, field, field, slots),
        in_specs=[vmem] * 13,
        out_specs=(vmem,) * 4,
        scratch_shapes=[
            pltpu.VMEM((rows + 2 * halo, 2 * y_cols), jnp.float32),
            pltpu.VMEM((rows, 2 * y_cols), jnp.float32),
            pltpu.VMEM((STEPS, rows, y_cols), jnp.float32),
            pltpu.VMEM((STEPS - 1, rows, y_cols), jnp.float32),
            pltpu.VMEM((STEPS, rows, y_cols), jnp.float32),
            pltpu.VMEM((devices,) + records.shape, jnp.float32),
            pltpu.VMEM((rows, total), jnp.bfloat16),
            pltpu.VMEM((3 * y_cols, total), jnp.bfloat16),
            pltpu.VMEM((rows, y_cols), jnp.float32),
            pltpu.VMEM((STEPS, 2, halo, 2 * y_cols), jnp.float32),
            pltpu.VMEM((STEPS, 2, halo, 2 * y_cols), jnp.float32),
            pltpu.VMEM((STEPS, 2, 8, rows), jnp.float32),
            pltpu.VMEM((STEPS, 2, 8, rows), jnp.float32),
            pltpu.SemaphoreType.DMA((STEPS, 4)),
            pltpu.SemaphoreType.DMA((STEPS, 4)),
            pltpu.SemaphoreType.DMA((devices,)),
            pltpu.SemaphoreType.DMA((devices,)),
            pltpu.SemaphoreType.DMA,
            pltpu.VMEM(slots.shape, jnp.float32),
            pltpu.SemaphoreType.DMA((z_depth,)),
            pltpu.SemaphoreType.DMA((z_depth,)),
            pltpu.SemaphoreType.DMA,
        ],
        compiler_params=pltpu.CompilerParams(
            collective_id=0, has_side_effects=True, vmem_limit_bytes=56 * 2**20
        ),
    )(model, u_prev, u_cur, a_next, a_cur, records, mass, *tables)


def halves(value):
    high = value.astype(jnp.bfloat16)
    return high, (value - high.astype(jnp.float32)).astype(jnp.bfloat16)


def dot_halves(left, right, right_dim=0):
    def product(a, b):
        return lax.dot_general(
            a, b, (((1,), (right_dim,)), ((), ())), preferred_element_type=jnp.float32
        )

    return product(left[0], right[0]) + (product(left[0], right[1]) + product(left[1], right[0]))


def spectral_kernel(
    grad_ref, mass_ref, x_high_ref, x_low_ref, y_high_ref, y_low_ref,
    out_ref,
    arrived, spectrum, y_high, y_low, back_high, back_low, leaving, partial,
    send_one, recv_one, send_two, recv_two, table_sem,
):
    chain = lax.axis_index("chain")
    tile = lax.axis_index("gx")
    devices = lax.axis_size("gx")
    planes, x_rows, y_cols = grad_ref.shape
    x_total = spectrum.shape[0]
    width = spectrum.shape[1] // 2
    plane, part = plane_and_part(tile, planes)

    loads = [
        pltpu.make_async_copy(y_high_ref.at[part], y_high, table_sem.at[0]),
        pltpu.make_async_copy(y_low_ref.at[part], y_low, table_sem.at[1]),
    ]
    for load in loads:
        load.start()
    barrier = pltpu.get_barrier_semaphore()

    @pl.loop(1, devices)
    def _(step):
        pl.semaphore_signal(
            barrier, inc=1, device_id=(chain, lax.rem(tile + step, devices)), device_id_type=MESH
        )

    def outward(step):
        peer = lax.rem(tile + step, devices)
        return pltpu.make_async_remote_copy(
            src_ref=grad_ref.at[plane_and_part(peer, planes)[0]],
            dst_ref=arrived.at[step],
            send_sem=send_one.at[step],
            recv_sem=recv_one.at[step],
            device_id=(chain, peer),
            device_id_type=MESH,
        )

    def homeward(step):
        return pltpu.make_async_remote_copy(
            src_ref=leaving.at[step],
            dst_ref=partial.at[step],
            send_sem=send_two.at[step],
            recv_sem=recv_two.at[step],
            device_id=(chain, lax.rem(tile + step, devices)),
            device_id_type=MESH,
        )

    spectrum[...] = jnp.zeros(spectrum.shape, jnp.float32)
    pl.semaphore_wait(barrier, devices - 1)

    @pl.loop(1, devices)
    def _(step):
        outward(step).start()

    for load in loads:
        load.wait()

    def block_rows(owner):
        return pl.ds(pl.multiple_of(owner // GY * x_rows, x_rows), x_rows)

    def table_rows(owner):
        return pl.ds(pl.multiple_of(lax.rem(owner, GY) * y_cols, y_cols), y_cols)

    def transform(owner, value):
        lines = table_rows(owner)
        spectrum[block_rows(owner), :] += dot_halves(
            halves(value), (y_high[lines, :], y_low[lines, :])
        )

    transform(tile, grad_ref[plane])

    @pl.loop(1, devices)
    def _(step):
        outward(step).wait_recv()
        transform(lax.rem(tile + devices - step, devices), arrived[step])

    def along_x(value, orient):
        mixed = dot_halves((x_high_ref[...], x_low_ref[...]), halves(value))
        cosine, sine = mixed[0:x_total], mixed[x_total:]
        real = cosine[:, 0:width] - orient * sine[:, width:]
        imag = cosine[:, width:] + orient * sine[:, 0:width]
        return real, imag

    real, imag = along_x(spectrum[...], -1.0)
    spectrum[:, 0:width] = real * mass_ref[...]
    spectrum[:, width:] = imag * mass_ref[...]
    real, imag = along_x(spectrum[...], 1.0)
    back_high[:, 0:width], back_low[:, 0:width] = halves(real)
    back_high[:, width:], back_low[:, width:] = halves(imag)

    def restored(owner):
        rows, lines = block_rows(owner), table_rows(owner)
        return dot_halves(
            (back_high[rows, :], back_low[rows, :]), (y_high[lines, :], y_low[lines, :]), 1
        )

    @pl.loop(1, devices)
    def _(step):
        leaving[step] = restored(lax.rem(tile + step, devices))
        homeward(step).start()

    out_ref[...] = jnp.zeros(out_ref.shape, jnp.float32)
    out_ref[plane] += restored(tile)

    @pl.loop(1, devices)
    def _(step):
        homeward(step).wait_recv()
        sender = lax.rem(tile + devices - step, devices)
        out_ref[plane_and_part(sender, planes)[0]] += partial[step]

    @pl.loop(1, devices)
    def _(step):
        outward(step).wait_send()
        homeward(step).wait_send()


def table_halves(table):
    high = table.astype(jnp.bfloat16)
    low = (table - high.astype(np.float64)).astype(jnp.bfloat16)
    return jnp.asarray(high), jnp.asarray(low)


def run_spectral(grad, mass):
    planes, x_rows, y_cols = grad.shape
    devices = lax.axis_size("gx")
    x_total, width = mass.shape
    y_total = y_cols * GY
    parts = y_total // width
    turn = np.arange(x_total)[:, None] * np.arange(x_total)[None, :] % x_total
    angle = turn * (2.0 * np.pi / x_total)
    x_tables = table_halves(np.concatenate((np.cos(angle), np.sin(angle)), axis=0))
    turn = np.arange(y_total)[:, None] * np.arange(y_total)[None, :] % y_total
    angle = (turn * (2.0 * np.pi / y_total)).reshape(y_total, parts, width).transpose(1, 0, 2)
    y_tables = table_halves(np.concatenate((np.cos(angle), -np.sin(angle)), axis=2))
    vmem = pl.BlockSpec(memory_space=pltpu.VMEM)
    hbm = pl.BlockSpec(memory_space=pl.ANY)
    tiles = (devices, x_rows, y_cols)
    return pl.pallas_call(
        spectral_kernel,
        out_shape=jax.ShapeDtypeStruct(grad.shape, jnp.float32),
        in_specs=[vmem] * 4 + [hbm] * 2,
        out_specs=vmem,
        scratch_shapes=[
            pltpu.VMEM(tiles, jnp.float32),
            pltpu.VMEM((x_total, 2 * width), jnp.float32),
            pltpu.VMEM((y_total, 2 * width), jnp.bfloat16),
            pltpu.VMEM((y_total, 2 * width), jnp.bfloat16),
            pltpu.VMEM((x_total, 2 * width), jnp.bfloat16),
            pltpu.VMEM((x_total, 2 * width), jnp.bfloat16),
            pltpu.VMEM(tiles, jnp.float32),
            pltpu.VMEM(tiles, jnp.float32),
            pltpu.SemaphoreType.DMA((devices,)),
            pltpu.SemaphoreType.DMA((devices,)),
            pltpu.SemaphoreType.DMA((devices,)),
            pltpu.SemaphoreType.DMA((devices,)),
            pltpu.SemaphoreType.DMA((2,)),
        ],
        compiler_params=pltpu.CompilerParams(
            collective_id=1, has_side_effects=True, vmem_limit_bytes=48 * 2**20
        ),
    )(grad, mass, *x_tables, *y_tables)


def pick_factor(length):
    candidate = math.isqrt(length)
    if candidate * candidate < length:
        candidate = candidate + 1
    while length % candidate != 0:
        candidate = candidate + 1
    return candidate


def phase_tables(rows_count, cols_count, modulus):
    first = jnp.arange(rows_count, dtype=jnp.int32)
    second = jnp.arange(cols_count, dtype=jnp.int32)
    phase_int = first[:, None] * second[None, :] % modulus
    angle_rad = phase_int.astype(jnp.float32) * (2.0 * math.pi / modulus)
    return (jnp.cos(angle_rad), jnp.sin(angle_rad))


def complex_mix(form, tab_cos, tab_sin, real_part, imag_part, orient):

    def product(table, data):
        return jnp.einsum(
            form, table, data, precision=lax.Precision.HIGHEST, preferred_element_type=jnp.float32
        )

    out_real = product(tab_cos, real_part) - orient * product(tab_sin, imag_part)
    out_imag = product(tab_cos, imag_part) + orient * product(tab_sin, real_part)
    return (out_real, out_imag)


def transform_rows(real_part, imag_part, orient):
    length, width = real_part.shape
    outer_len = pick_factor(length)
    inner_len = length // outer_len
    data_re = real_part.reshape(outer_len, inner_len, width)
    data_im = imag_part.reshape(outer_len, inner_len, width)
    cos_outer, sin_outer = phase_tables(outer_len, outer_len, outer_len)
    mid_re, mid_im = complex_mix("ca,abm->cbm", cos_outer, sin_outer, data_re, data_im, orient)
    twist_cos, twist_sin = phase_tables(outer_len, inner_len, length)
    twist_cos = twist_cos[:, :, None]
    twist_sin = twist_sin[:, :, None]
    turned_re = mid_re * twist_cos - orient * mid_im * twist_sin
    turned_im = mid_im * twist_cos + orient * mid_re * twist_sin
    cos_inner, sin_inner = phase_tables(inner_len, inner_len, inner_len)
    final_re, final_im = complex_mix(
        "db,cbm->dcm", cos_inner, sin_inner, turned_re, turned_im, orient
    )
    return (final_re.reshape(length, width), final_im.reshape(length, width))


def per_device(
    courant, ckpt_prev, ckpt_cur, adj_next, adj_cur, rec_x, rec_plane, traces, mass_kernel
):
    x_rows, z_depth, y_cols = courant.shape[1:]
    devices = lax.axis_size("gx")
    x_blocks = devices // GY
    x_total = x_rows * x_blocks
    y_total = y_cols * GY
    cell_y = rec_plane % y_total
    cell_z = rec_plane // y_total
    owner = rec_x // x_rows * GY + cell_y // y_cols
    cell_row = (owner * x_rows + rec_x % x_rows) * z_depth + cell_z
    records = jnp.concatenate(
        (
            cell_row.astype(jnp.float32)[None],
            (cell_y % y_cols).astype(jnp.float32)[None],
            traces,
            jnp.zeros((6 - STEPS, rec_x.shape[0]), jnp.float32),
        ),
        axis=0,
    )
    dense = x_total <= 512 and GY % z_depth == 0 and devices % z_depth == 0
    mass = mass_kernel.reshape(-1, 128) if dense else jnp.zeros((8, 128), jnp.float32)
    gradient, adj_now, adj_later, mass_slots = run_window(
        *(
            field.reshape(x_rows * z_depth, y_cols)
            for field in (courant, ckpt_prev, ckpt_cur, adj_next, adj_cur)
        ),
        records,
        mass,
        dense,
    )
    tile_shape = (1, x_rows, z_depth, y_cols)
    if dense:
        by_plane = gradient.reshape(x_rows, z_depth, y_cols).transpose(1, 0, 2)
        part_mass = mass_slots.reshape(z_depth, x_total, -1).transpose(1, 0, 2)
        part_mass = part_mass.reshape(x_total, -1) * (1.0 / (x_total * y_total))
        scaled = run_spectral(by_plane, part_mass).transpose(1, 0, 2)
        return (
            scaled.reshape(tile_shape),
            adj_now.reshape(tile_shape),
            adj_later.reshape(tile_shape),
        )
    flat_grad = gradient.reshape(x_rows * z_depth, 1, y_cols)
    rows = lax.all_to_all(flat_grad, "gx", split_axis=0, concat_axis=1, tiled=True)
    share = rows.shape[0]
    lines = rows.reshape(share * x_blocks, y_total).T
    spec_re_t, spec_im_t = transform_rows(lines, jnp.zeros_like(lines), -1.0)
    spec_re = spec_re_t.T.reshape(share, x_blocks, y_total)
    spec_im = spec_im_t.T.reshape(share, x_blocks, y_total)
    cols_re, cols_im = (
        lax.all_to_all(spec_re, "gx", split_axis=2, concat_axis=0, tiled=True),
        lax.all_to_all(spec_im, "gx", split_axis=2, concat_axis=0, tiled=True),
    )
    col_width = cols_re.shape[2]
    half_width = z_depth * col_width

    def to_columns(part):
        return (
            part.reshape(x_rows, z_depth, x_blocks, col_width)
            .transpose(2, 0, 1, 3)
            .reshape(x_total, half_width)
        )

    def from_columns(part):
        return (
            part.reshape(x_blocks, x_rows, z_depth, col_width)
            .transpose(1, 2, 0, 3)
            .reshape(devices * share, x_blocks, col_width)
        )

    freq_re, freq_im = transform_rows(to_columns(cols_re), to_columns(cols_im), -1.0)
    kernel_scale = (
        jnp.broadcast_to(mass_kernel[:, None, :], (x_total, z_depth, col_width)).reshape(
            x_total, half_width
        )
        / x_total
    )
    freq_re = freq_re * kernel_scale
    freq_im = freq_im * kernel_scale
    spat_re, spat_im = transform_rows(freq_re, freq_im, 1.0)
    back_re = from_columns(spat_re)
    back_im = from_columns(spat_im)
    line_re, line_im = (
        lax.all_to_all(back_re, "gx", split_axis=0, concat_axis=2, tiled=True),
        lax.all_to_all(back_im, "gx", split_axis=0, concat_axis=2, tiled=True),
    )
    lines_re = line_re.reshape(share * x_blocks, y_total).T
    lines_im = line_im.reshape(share * x_blocks, y_total).T
    real_t, imag_t = transform_rows(lines_re, lines_im, 1.0)
    real_lines = (real_t.T / y_total).reshape(share, devices, y_cols)
    tiled = lax.all_to_all(real_lines, "gx", split_axis=1, concat_axis=0, tiled=True)
    return (tiled.reshape(tile_shape), adj_now.reshape(tile_shape), adj_later.reshape(tile_shape))


def solution(mesh):
    in_specs = (
        P(("chain", "gx"), None, None, None),
        P(("chain", "gx"), None, None, None),
        P(("chain", "gx"), None, None, None),
        P(("chain", "gx"), None, None, None),
        P(("chain", "gx"), None, None, None),
        P(("chain", "gx")),
        P(("chain", "gx")),
        P(None, ("chain", "gx")),
        P(None, "gx"),
    )
    out_specs = (
        P(("chain", "gx"), None, None, None),
        P(("chain", "gx"), None, None, None),
        P(("chain", "gx"), None, None, None),
    )
    return jax.shard_map(
        per_device, mesh=mesh, in_specs=in_specs, out_specs=out_specs, check_vma=False
    )
```

profile of v0, /device:TPU:31, one launch (start us, length us, event | category | flops | bytes accessed | tf_op | source)
XLA Modules:
  0.0 99.7 jit_solution(13785042354970438303)
XLA Ops:
  0.6 0.0 copy-start.1
  0.6 0.0 copy-start.2
  0.7 0.1 pad.3.clone
  0.7 0.7 convert_bitcast_fusion
  1.5 1.3 %maximum_maximum_fusion.rec_ref = f32[8,128]{1,0:T(8,128)} fusion(f32[4,128]{1,0:T(4,128)} %param.26, f32[1,128]{1,0:T(1,128)S(1)} %fusion.2, f32[1,128]{1,0:T(1,128)S(1)} %get-tuple-element.17, f32[8]{0:T(128)S(1)} %pad.3.clone), kind=kLoop, calls=%fused_computation.2 | loop fusion | flops 3072 | bytes 7200 | tf_op jit(solution)/shard_map/concatenate | solution.py:592
  2.8 0.9 copy.25
  3.8 0.7 reshape.47.mass_ref
  4.5 33.8 %shard_map.202 = (f32[512,128]{1,0:T(8,128)}, f32[512,128]{1,0:T(8,128)}, f32[512,128]{1,0:T(8,128)}, f32[4,128,128]{2,1,0:T(8,128)}) custom-call(f32[512,128]{1,0:T(8,128)} %bitcast.24, f32[512,128]{1,0:T(8,128)} %bitcast.25, f32[512,128]{1,0:T(8,128)} %bitcast.26, f32[512,128]{1,0:T(8,128)} %bitcast.27, f32[512,128]{1,0:T(8,128)} %bitcast.28, ...), custom_call_target="tpu_custom_call" | custom-call | tf_op jit(solution)/shard_map/pallas_call | solution.py:317
  38.3 1.0 copy.31
  39.3 1.0 broadcast_multiply_fusion
  40.2 0.1 mul.35
  40.4 0.2 copy.27
  40.6 0.1 copy.28.mass_ref
  40.7 0.0 copy-done.1
  40.7 0.0 copy-done.2
  40.7 0.0 copy-start
  40.7 2.2 %copy-done = bf16[4,1024,512]{2,1,0:T(8,128)(2,1)S(1)} copy-done((bf16[4,1024,512]{2,1,0:T(8,128)(2,1)S(1)}, bf16[4,1024,512]{2,1,0:T(8,128)(2,1)}, u32[]{:S(2)}) %copy-start) | copy-done | bytes 4194328
  42.9 0.0 copy-start.4
  42.9 54.4 %shard_map.203 = f32[4,128,128]{2,1,0:T(8,128)S(1)} custom-call(f32[4,128,128]{2,1,0:T(8,128)S(1)} %bitcast.20, f32[256,256]{1,0:T(8,128)S(1)} %copy.28.mass_ref, bf16[512,256]{1,0:T(8,128)(2,1)S(1)} %copy-done.2, bf16[512,256]{1,0:T(8,128)(2,1)S(1)} %copy-done.1, bf16[4,1024,512]{2,1,0:T(8,128)(2,1)S(1)} %copy-done, ...), custom_call_target="tpu_custom_call" | custom-call | tf_op jit(solution)/shard_map/pallas_call | solution.py:505
  97.4 0.9 copy.29
  98.3 0.0 copy-done.4
  98.3 0.7 copy.34
  99.0 0.0 copy-done.3
  99.0 0.7 copy.35
  (3 shorter events, 0.0 us)
Async XLA Ops:
  0.6 40.1 %copy-start.1 = (bf16[512,256]{1,0:T(8,128)(2,1)S(1)}, bf16[512,256]{1,0:T(8,128)(2,1)}, u32[]{:S(2)}) copy-start(bf16[512,256]{1,0:T(8,128)(2,1)} %constant.96.clone.x_low_ref) | copy-start | bytes 786436
  0.6 40.1 %copy-start.2 = (bf16[512,256]{1,0:T(8,128)(2,1)S(1)}, bf16[512,256]{1,0:T(8,128)(2,1)}, u32[]{:S(2)}) copy-start(bf16[512,256]{1,0:T(8,128)(2,1)} %constant.95.clone.x_high_ref) | copy-start | bytes 786436
  40.7 2.2 %copy-start = (bf16[4,1024,512]{2,1,0:T(8,128)(2,1)S(1)}, bf16[4,1024,512]{2,1,0:T(8,128)(2,1)}, u32[]{:S(2)}) copy-start(bf16[4,1024,512]{2,1,0:T(8,128)(2,1)} %constant.97.clone.y_high_ref) | copy-start | bytes 12582916
  42.9 55.3 %copy-start.4 = (f32[512,128]{1,0:T(8,128)S(1)}, f32[512,128]{1,0:T(8,128)}, u32[]{:S(2)}) copy-start(f32[512,128]{1,0:T(8,128)} %get-tuple-element.9) | copy-start | bytes 786436
  42.9 56.0 %copy-start.3 = (f32[512,128]{1,0:T(8,128)S(1)}, f32[512,128]{1,0:T(8,128)}, u32[]{:S(2)}) copy-start(f32[512,128]{1,0:T(8,128)} %get-tuple-element.10) | copy-start | bytes 786436
where the time goes:
time: 100 us; the launch traced here: 99.7 us
  Pallas kernels  88.2 us (88%)
  local copies, waits for them, and re-layouts  7.63 us (8%)
  other arithmetic  3.06 us (3%)
    pallas_call x1, Pallas kernels, run_spectral(): pl.pallas_call(spectral_kernel, out_shape=jax.ShapeDtypeStruct(grad.shape...  54.4 us
    pallas_call x1, Pallas kernels, run_window(): pl.pallas_call(functools.partial(window_kernel, chunk, move_mass), out_sh...  33.8 us
    unnamed x14, local copies, waits for them, and re-layouts  5.41 us

commit v1 on v0

--- a/solution.py
+++ b/solution.py
@@ -122,6 +122,9 @@
     low_rows = lax.broadcasted_iota(jnp.int32, rim_ref.shape, 0) < 8
     rim = rim_ref[...] * jnp.where(low_rows, has_left, has_right)
 
+    along = halves(along_ref[...])
+    band = halves(band_ref[...])
+
     def pack(phase, wave, adjoint):
         both[halo : halo + rows, 0:y_cols] = wave
         both[halo : halo + rows, y_cols:] = model_ref[...] * adjoint
@@ -217,11 +220,13 @@
             if move_mass:
                 mass_start()
 
-        lap[...] = dot_f32(both[halo : halo + rows, :], along_ref[...])
+        high, low = halves(both[...])
         for start in range(0, rows, chunk):
-            lap[start : start + chunk, :] += dot_f32(
-                band_ref[...], both[start : start + chunk + 2 * halo, :]
-            )
+            inner = slice(halo + start, halo + start + chunk)
+            outer = slice(start, start + chunk + 2 * halo)
+            lap[start : start + chunk, :] = dot_halves(
+                (high[inner], low[inner]), along
+            ) + dot_halves(band, (high[outer], low[outer]))
         if phase == 0:
             own.wait()
 
@@ -245,23 +250,19 @@
             value = records[step, 2 + section : 3 + section, :]
             index = lax.broadcasted_iota(jnp.int32, (y_cols, width), 0).astype(jnp.float32)
             rest = jnp.where(index == place, value, 0.0)
-            for level in range(3):
+            for level in range(2):
                 piece = rest.astype(jnp.bfloat16)
                 weights[level * y_cols : (level + 1) * y_cols, lanes] = piece
                 rest = rest - piece.astype(jnp.float32)
 
         def injected(lanes):
-            triple = lax.dot_general(
+            pair = lax.dot_general(
                 hot[:, lanes],
                 weights[:, lanes],
                 (((1,), (1,)), ((), ())),
                 preferred_element_type=jnp.float32,
             )
-            return (
-                triple[:, 0:y_cols]
-                + triple[:, y_cols : 2 * y_cols]
-                + triple[:, 2 * y_cols :]
-            )
+            return pair[:, 0:y_cols] + pair[:, y_cols:]
 
         inject[...] = injected(pl.ds(0, part))
         if total > part:
@@ -327,7 +328,7 @@
             pltpu.VMEM((STEPS, rows, y_cols), jnp.float32),
             pltpu.VMEM((devices,) + records.shape, jnp.float32),
             pltpu.VMEM((rows, total), jnp.bfloat16),
-            pltpu.VMEM((3 * y_cols, total), jnp.bfloat16),
+            pltpu.VMEM((2 * y_cols, total), jnp.bfloat16),
             pltpu.VMEM((rows, y_cols), jnp.float32),
             pltpu.VMEM((STEPS, 2, halo, 2 * y_cols), jnp.float32),
             pltpu.VMEM((STEPS, 2, halo, 2 * y_cols), jnp.float32),
@@ -391,34 +392,58 @@
             barrier, inc=1, device_id=(chain, lax.rem(tile + step, devices)), device_id_type=MESH
         )
 
-    def outward(step):
-        peer = lax.rem(tile + step, devices)
+    sibling = tile + 1 - 2 * lax.rem(tile, 2)
+    turns = devices // 2
+
+    def copy_to(peer, source, target, send_sem, recv_sem):
         return pltpu.make_async_remote_copy(
-            src_ref=grad_ref.at[plane_and_part(peer, planes)[0]],
-            dst_ref=arrived.at[step],
-            send_sem=send_one.at[step],
-            recv_sem=recv_one.at[step],
+            src_ref=source,
+            dst_ref=target,
+            send_sem=send_sem,
+            recv_sem=recv_sem,
             device_id=(chain, peer),
             device_id_type=MESH,
         )
 
-    def homeward(step):
-        return pltpu.make_async_remote_copy(
-            src_ref=leaving.at[step],
-            dst_ref=partial.at[step],
-            send_sem=send_two.at[step],
-            recv_sem=recv_two.at[step],
-            device_id=(chain, lax.rem(tile + step, devices)),
-            device_id_type=MESH,
+    def ahead(first, turn):
+        return lax.rem(first + 2 * turn, devices)
+
+    def behind(first, turn):
+        return lax.rem(first + devices - 2 * turn, devices)
+
+    def outward(turn):
+        peer = ahead(tile, turn)
+        slot = 2 * turn
+        source = grad_ref.at[plane_and_part(peer, planes)[0]]
+        return copy_to(peer, source, arrived.at[slot], send_one.at[slot], recv_one.at[slot])
+
+    def forward(turn):
+        slot = 2 * turn + 1
+        return copy_to(
+            sibling, arrived.at[2 * turn], arrived.at[slot], send_one.at[slot], recv_one.at[slot]
+        )
+
+    def homeward(turn):
+        slot = 2 * turn
+        return copy_to(
+            ahead(tile, turn), leaving.at[slot], partial.at[slot], send_two.at[slot], recv_two.at[slot]
+        )
+
+    def across(turn):
+        slot = 2 * turn + 1
+        return copy_to(
+            sibling, leaving.at[slot], partial.at[slot], send_two.at[slot], recv_two.at[slot]
         )
 
     spectrum[...] = jnp.zeros(spectrum.shape, jnp.float32)
     pl.semaphore_wait(barrier, devices - 1)
 
-    @pl.loop(1, devices)
-    def _(step):
-        outward(step).start()
-
+    @pl.loop(1, turns)
+    def _(turn):
+        outward(turn).start()
+
+    arrived[0] = grad_ref[plane]
+    forward(0).start()
     for load in loads:
         load.wait()
 
@@ -436,10 +461,18 @@
 
     transform(tile, grad_ref[plane])
 
-    @pl.loop(1, devices)
-    def _(step):
-        outward(step).wait_recv()
-        transform(lax.rem(tile + devices - step, devices), arrived[step])
+    def take_forwarded(turn):
+        forward(turn).wait_recv()
+        transform(behind(sibling, turn), arrived[2 * turn + 1])
+
+    @pl.loop(1, turns)
+    def _(turn):
+        outward(turn).wait_recv()
+        forward(turn).start()
+        transform(behind(tile, turn), arrived[2 * turn])
+        take_forwarded(turn - 1)
+
+    take_forwarded(turns - 1)
 
     def along_x(value, orient):
         mixed = dot_halves((x_high_ref[...], x_low_ref[...]), halves(value))
@@ -461,24 +494,39 @@
             (back_high[rows, :], back_low[rows, :]), (y_high[lines, :], y_low[lines, :]), 1
         )
 
-    @pl.loop(1, devices)
-    def _(step):
-        leaving[step] = restored(lax.rem(tile + step, devices))
-        homeward(step).start()
+    def pass_across(turn):
+        leaving[2 * turn + 1] = restored(ahead(sibling, turn))
+        across(turn).start()
+
+    pass_across(1)
+
+    @pl.loop(1, turns)
+    def _(turn):
+        pass_across(lax.rem(turn + 1, turns))
+        own = restored(ahead(tile, turn))
+        across(turn).wait_recv()
+        leaving[2 * turn] = own + partial[2 * turn + 1]
+        homeward(turn).start()
 
     out_ref[...] = jnp.zeros(out_ref.shape, jnp.float32)
-    out_ref[plane] += restored(tile)
-
-    @pl.loop(1, devices)
-    def _(step):
-        homeward(step).wait_recv()
-        sender = lax.rem(tile + devices - step, devices)
-        out_ref[plane_and_part(sender, planes)[0]] += partial[step]
-
-    @pl.loop(1, devices)
-    def _(step):
-        outward(step).wait_send()
-        homeward(step).wait_send()
+    mine = restored(tile)
+    across(0).wait_recv()
+    out_ref[plane] += mine + partial[1]
+
+    @pl.loop(1, turns)
+    def _(turn):
+        homeward(turn).wait_recv()
+        out_ref[plane_and_part(behind(tile, turn), planes)[0]] += partial[2 * turn]
+
+    forward(0).wait_send()
+    across(0).wait_send()
+
+    @pl.loop(1, turns)
+    def _(turn):
+        outward(turn).wait_send()
+        forward(turn).wait_send()
+        across(turn).wait_send()
+        homeward(turn).wait_send()
 
 
 def table_halves(table):
@@ -598,7 +646,7 @@
         ),
         axis=0,
     )
-    dense = x_total <= 512 and GY % z_depth == 0 and devices % z_depth == 0
+    dense = x_total <= 512 and GY == 2 * z_depth and devices % z_depth == 0
     mass = mass_kernel.reshape(-1, 128) if dense else jnp.zeros((8, 128), jnp.float32)
     gradient, adj_now, adj_later, mass_slots = run_window(
         *(

time: 100 us -> 76.9 us (0.77)
  Pallas kernels: 88.2 us -> 65.1 us
    pallas_call x1, Pallas kernels: 54.4 us -> 37 us  [run_spectral(): pl.pallas_call(spectral_kernel, out_shape=jax.ShapeDtypeStruct(grad.shape...]
    pallas_call x1, Pallas kernels: 33.8 us -> 28.1 us  [run_window(): pl.pallas_call(functools.partial(window_kernel, chunk, move_mass), out_sh...]
where the time goes in v1:
time: 76.9 us; the launch traced here: 76.6 us
  Pallas kernels  65.1 us (85%)
  local copies, waits for them, and re-layouts  7.63 us (10%)
  other arithmetic  3.06 us (4%)
    pallas_call x1, Pallas kernels, run_spectral(): pl.pallas_call(spectral_kernel, out_shape=jax.ShapeDtypeStruct(grad.shape...  37 us
    pallas_call x1, Pallas kernels, run_window(): pl.pallas_call(functools.partial(window_kernel, chunk, move_mass), out_sh...  28.1 us
    unnamed x14, local copies, waits for them, and re-layouts  5.41 us

profile of v1, /device:TPU:31, one launch (start us, length us, event | category | flops | bytes accessed | tf_op | source)
XLA Modules:
  0.0 76.6 jit_solution(18418473125884325012)
XLA Ops:
  0.6 0.0 copy-start.1
  0.6 0.0 copy-start.2
  0.7 0.1 pad.3.clone
  0.7 0.7 convert_bitcast_fusion
  1.5 1.3 %maximum_maximum_fusion.rec_ref = f32[8,128]{1,0:T(8,128)} fusion(f32[4,128]{1,0:T(4,128)} %param.26, f32[1,128]{1,0:T(1,128)S(1)} %fusion.2, f32[1,128]{1,0:T(1,128)S(1)} %get-tuple-element.17, f32[8]{0:T(128)S(1)} %pad.3.clone), kind=kLoop, calls=%fused_computation.2 | loop fusion | flops 3072 | bytes 7200 | tf_op jit(solution)/shard_map/concatenate | solution.py:640
  2.8 0.9 %copy.25 = f32[256,64]{1,0:T(8,128)S(1)} copy(f32[256,64]{0,1:T(8,128)} %param.27) | data formatting | bytes 131072 | tf_op args[8]
  3.8 0.7 reshape.47.mass_ref
  4.5 28.1 %shard_map.202 = (f32[512,128]{1,0:T(8,128)}, f32[512,128]{1,0:T(8,128)}, f32[512,128]{1,0:T(8,128)}, f32[4,128,128]{2,1,0:T(8,128)}) custom-call(f32[512,128]{1,0:T(8,128)} %bitcast.24, f32[512,128]{1,0:T(8,128)} %bitcast.25, f32[512,128]{1,0:T(8,128)} %bitcast.26, f32[512,128]{1,0:T(8,128)} %bitcast.27, f32[512,128]{1,0:T(8,128)} %bitcast.28, ...), custom_call_target="tpu_custom_call" | custom-call | tf_op jit(solution)/shard_map/pallas_call | solution.py:318
  32.6 1.0 %copy.31 = f32[128,4,128]{2,0,1:T(8,128)S(1)} copy(f32[128,4,128]{2,1,0:T(4,128)} %bitcast.31) | data formatting | bytes 524288 | tf_op jit(solution)/shard_map/reshape | solution.py:662
  33.6 1.0 %broadcast_multiply_fusion = f32[4,128,128]{2,1,0:T(8,128)S(1)} fusion(f32[4,128,128]{2,1,0:T(8,128)} %get-tuple-element.8), kind=kLoop, calls=%fused_computation.1 | loop fusion | flops 65536 | bytes 524288 | tf_op jit(solution)/shard_map/mul | solution.py:664
  34.5 0.1 mul.35
  34.7 0.2 copy.27
  34.9 0.1 copy.28.mass_ref
  35.0 0.0 copy-done.1
  35.0 0.0 copy-done.2
  35.0 0.0 copy-start
  35.1 2.2 %copy-done = bf16[4,1024,512]{2,1,0:T(8,128)(2,1)S(1)} copy-done((bf16[4,1024,512]{2,1,0:T(8,128)(2,1)S(1)}, bf16[4,1024,512]{2,1,0:T(8,128)(2,1)}, u32[]{:S(2)}) %copy-start) | copy-done | bytes 4194328
  37.2 0.0 copy-start.4
  37.2 37.0 %shard_map.203 = f32[4,128,128]{2,1,0:T(8,128)S(1)} custom-call(f32[4,128,128]{2,1,0:T(8,128)S(1)} %bitcast.20, f32[256,256]{1,0:T(8,128)S(1)} %copy.28.mass_ref, bf16[512,256]{1,0:T(8,128)(2,1)S(1)} %copy-done.2, bf16[512,256]{1,0:T(8,128)(2,1)S(1)} %copy-done.1, bf16[4,1024,512]{2,1,0:T(8,128)(2,1)S(1)} %copy-done, ...), custom_call_target="tpu_custom_call" | custom-call | tf_op jit(solution)/shard_map/pallas_call | solution.py:553
  74.3 0.9 %copy.29 = f32[1,128,4,128]{3,2,1,0:T(4,128)} copy(f32[1,128,4,128]{3,1,2,0:T(8,128)S(1)} %bitcast.21) | data formatting | bytes 524288
  75.2 0.0 copy-done.4
  75.2 0.7 copy.34
  75.9 0.0 copy-done.3
  75.9 0.7 copy.35
  (3 shorter events, 0.0 us)
Async XLA Ops:
  0.6 34.4 %copy-start.1 = (bf16[512,256]{1,0:T(8,128)(2,1)S(1)}, bf16[512,256]{1,0:T(8,128)(2,1)}, u32[]{:S(2)}) copy-start(bf16[512,256]{1,0:T(8,128)(2,1)} %constant.96.clone.x_low_ref) | copy-start | bytes 786436
  0.6 34.4 %copy-start.2 = (bf16[512,256]{1,0:T(8,128)(2,1)S(1)}, bf16[512,256]{1,0:T(8,128)(2,1)}, u32[]{:S(2)}) copy-start(bf16[512,256]{1,0:T(8,128)(2,1)} %constant.95.clone.x_high_ref) | copy-start | bytes 786436
  35.0 2.2 %copy-start = (bf16[4,1024,512]{2,1,0:T(8,128)(2,1)S(1)}, bf16[4,1024,512]{2,1,0:T(8,128)(2,1)}, u32[]{:S(2)}) copy-start(bf16[4,1024,512]{2,1,0:T(8,128)(2,1)} %constant.97.clone.y_high_ref) | copy-start | bytes 12582916
  37.2 37.9 %copy-start.4 = (f32[512,128]{1,0:T(8,128)S(1)}, f32[512,128]{1,0:T(8,128)}, u32[]{:S(2)}) copy-start(f32[512,128]{1,0:T(8,128)} %get-tuple-element.9) | copy-start | bytes 786436
  37.2 38.6 %copy-start.3 = (f32[512,128]{1,0:T(8,128)S(1)}, f32[512,128]{1,0:T(8,128)}, u32[]{:S(2)}) copy-start(f32[512,128]{1,0:T(8,128)} %get-tuple-element.10) | copy-start | bytes 786436

commit v2 on v1

--- a/solution.py
+++ b/solution.py
@@ -130,9 +130,20 @@
         both[halo : halo + rows, y_cols:] = model_ref[...] * adjoint
         x_out[phase, 0] = both[halo : 2 * halo, :]
         x_out[phase, 1] = both[rows : halo + rows, :]
-        strips = dot_f32(pick_ref[...], both[halo : halo + rows, :], 1, 1)
+        high, low = halves(both[...])
+        picked = pick_ref[...].astype(jnp.bfloat16)
+        strips = sum(
+            lax.dot_general(
+                picked,
+                level[halo : halo + rows],
+                (((1,), (1,)), ((), ())),
+                preferred_element_type=jnp.float32,
+            )
+            for level in (high, low)
+        )
         y_out[phase, 0] = strips[0:8]
         y_out[phase, 1] = strips[8:16]
+        return high, low
 
     def halo_copies(phase):
         copies = []
@@ -200,7 +211,7 @@
             pl.when(quarter * slots + slot != tile)(arrival.wait_recv)
         mass_out[...] = mass_in[...]
 
-    pack(0, cur_ref[...], now_ref[...])
+    high, low = pack(0, cur_ref[...], now_ref[...])
     pl.semaphore_wait(barrier, devices - 1)
     pending = []
     width = rec_ref.shape[1]
@@ -220,7 +231,6 @@
             if move_mass:
                 mass_start()
 
-        high, low = halves(both[...])
         for start in range(0, rows, chunk):
             inner = slice(halo + start, halo + start + chunk)
             outer = slice(start, start + chunk + 2 * halo)
@@ -287,7 +297,7 @@
         now = now_ref[...] if phase == 0 else adjoints[phase - 1]
         adjoints[phase] = 2.0 * now - later + lap[:, y_cols:] + inject[...]
         if phase + 1 < STEPS:
-            pack(phase + 1, waves[phase], adjoints[phase])
+            high, low = pack(phase + 1, waves[phase], adjoints[phase])
     grad_ref[...] = (
         now_ref[...] * images[3]
         + adjoints[0] * images[2]
@@ -365,9 +375,9 @@
 
 
 def spectral_kernel(
-    grad_ref, mass_ref, x_high_ref, x_low_ref, y_high_ref, y_low_ref,
+    grad_ref, mass_ref, x_high_ref, x_low_ref, y_ref,
     out_ref,
-    arrived, spectrum, y_high, y_low, back_high, back_low, leaving, partial,
+    arrived, spectrum, y_table, y_high, y_low, back_high, back_low, leaving, partial,
     send_one, recv_one, send_two, recv_two, table_sem,
 ):
     chain = lax.axis_index("chain")
@@ -378,12 +388,8 @@
     width = spectrum.shape[1] // 2
     plane, part = plane_and_part(tile, planes)
 
-    loads = [
-        pltpu.make_async_copy(y_high_ref.at[part], y_high, table_sem.at[0]),
-        pltpu.make_async_copy(y_low_ref.at[part], y_low, table_sem.at[1]),
-    ]
-    for load in loads:
-        load.start()
+    load = pltpu.make_async_copy(y_ref.at[part], y_table, table_sem)
+    load.start()
     barrier = pltpu.get_barrier_semaphore()
 
     @pl.loop(1, devices)
@@ -444,8 +450,8 @@
 
     arrived[0] = grad_ref[plane]
     forward(0).start()
-    for load in loads:
-        load.wait()
+    load.wait()
+    y_high[...], y_low[...] = halves(y_table[...])
 
     def block_rows(owner):
         return pl.ds(pl.multiple_of(owner // GY * x_rows, x_rows), x_rows)
@@ -546,18 +552,19 @@
     x_tables = table_halves(np.concatenate((np.cos(angle), np.sin(angle)), axis=0))
     turn = np.arange(y_total)[:, None] * np.arange(y_total)[None, :] % y_total
     angle = (turn * (2.0 * np.pi / y_total)).reshape(y_total, parts, width).transpose(1, 0, 2)
-    y_tables = table_halves(np.concatenate((np.cos(angle), -np.sin(angle)), axis=2))
+    y_table = np.concatenate((np.cos(angle), -np.sin(angle)), axis=2).astype(np.float32)
     vmem = pl.BlockSpec(memory_space=pltpu.VMEM)
     hbm = pl.BlockSpec(memory_space=pl.ANY)
     tiles = (devices, x_rows, y_cols)
     return pl.pallas_call(
         spectral_kernel,
         out_shape=jax.ShapeDtypeStruct(grad.shape, jnp.float32),
-        in_specs=[vmem] * 4 + [hbm] * 2,
+        in_specs=[vmem] * 4 + [hbm],
         out_specs=vmem,
         scratch_shapes=[
             pltpu.VMEM(tiles, jnp.float32),
             pltpu.VMEM((x_total, 2 * width), jnp.float32),
+            pltpu.VMEM((y_total, 2 * width), jnp.float32),
             pltpu.VMEM((y_total, 2 * width), jnp.bfloat16),
             pltpu.VMEM((y_total, 2 * width), jnp.bfloat16),
             pltpu.VMEM((x_total, 2 * width), jnp.bfloat16),
@@ -568,12 +575,12 @@
             pltpu.SemaphoreType.DMA((devices,)),
             pltpu.SemaphoreType.DMA((devices,)),
             pltpu.SemaphoreType.DMA((devices,)),
-            pltpu.SemaphoreType.DMA((2,)),
+            pltpu.SemaphoreType.DMA,
         ],
         compiler_params=pltpu.CompilerParams(
-            collective_id=1, has_side_effects=True, vmem_limit_bytes=48 * 2**20
+            collective_id=1, has_side_effects=True, vmem_limit_bytes=60 * 2**20
         ),
-    )(grad, mass, *x_tables, *y_tables)
+    )(grad, mass, *x_tables, jnp.asarray(y_table))
 
 
 def pick_factor(length):

time: 76.9 us -> 78.3 us (1.018)
  Pallas kernels: 65.1 us -> 66.4 us
    pallas_call x1, Pallas kernels: 37 us -> 38.7 us  [run_spectral(): pl.pallas_call(spectral_kernel, out_shape=jax.ShapeDtypeStruct(grad.shape...]
    unnamed x14 -> x8, local copies, waits for them, and re-layouts: 5.41 us -> 4.17 us
where the time goes in v2:
time: 78.3 us; the launch traced here: 78 us
  Pallas kernels  66.4 us (85%)
  local copies, waits for them, and re-layouts  7.85 us (10%)
  other arithmetic  3.01 us (4%)
    pallas_call x1, Pallas kernels, run_spectral(): pl.pallas_call(spectral_kernel, out_shape=jax.ShapeDtypeStruct(grad.shape...  38.7 us
    pallas_call x1, Pallas kernels, run_window(): pl.pallas_call(functools.partial(window_kernel, chunk, move_mass), out_sh...  27.7 us
    unnamed x8, local copies, waits for them, and re-layouts  4.17 us
    reshape x1, local copies, waits for them, and re-layouts, per_device(): by_plane = gradient.reshape(x_rows, z_depth, y_cols).transpose(1, 0, 2)  1.73 us

profile of v2, /device:TPU:31, one launch (start us, length us, event | category | flops | bytes accessed | tf_op | source)
XLA Modules:
  0.0 78.0 jit_solution(8254919498598672187)
XLA Ops:
  0.6 0.1 pad.3.clone
  0.7 0.7 convert_bitcast_fusion
  1.4 1.3 %maximum_maximum_fusion.rec_ref = f32[8,128]{1,0:T(8,128)} fusion(f32[4,128]{1,0:T(4,128)} %param.25, f32[1,128]{1,0:T(1,128)S(1)} %fusion.2, f32[1,128]{1,0:T(1,128)S(1)} %get-tuple-element.17, f32[8]{0:T(128)S(1)} %pad.3.clone), kind=kLoop, calls=%fused_computation.2 | loop fusion | flops 3072 | bytes 7200 | tf_op jit(solution)/shard_map/concatenate | solution.py:647
  2.8 0.9 %copy.24 = f32[256,64]{1,0:T(8,128)S(1)} copy(f32[256,64]{0,1:T(8,128)} %param.26) | data formatting | bytes 131072 | tf_op args[8]
  3.7 0.7 reshape.47.mass_ref
  4.4 27.7 %shard_map.193 = (f32[512,128]{1,0:T(8,128)}, f32[512,128]{1,0:T(8,128)}, f32[512,128]{1,0:T(8,128)}, f32[4,128,128]{2,1,0:T(8,128)}) custom-call(f32[512,128]{1,0:T(8,128)} %bitcast.24, f32[512,128]{1,0:T(8,128)} %bitcast.25, f32[512,128]{1,0:T(8,128)} %bitcast.26, f32[512,128]{1,0:T(8,128)} %bitcast.27, f32[512,128]{1,0:T(8,128)} %bitcast.28, ...), custom_call_target="tpu_custom_call" | custom-call | tf_op jit(solution)/shard_map/pallas_call | solution.py:328
  32.1 0.0 copy-start.1
  32.1 0.0 copy-start
  32.1 1.7 %copy.30 = f32[128,4,128]{2,0,1:T(8,128)} copy(f32[128,4,128]{2,1,0:T(4,128)} %bitcast.31) | data formatting | bytes 524288 | tf_op jit(solution)/shard_map/reshape | solution.py:669
  33.9 1.0 %broadcast_multiply_fusion = f32[4,128,128]{2,1,0:T(8,128)S(1)} fusion(f32[4,128,128]{2,1,0:T(8,128)} %get-tuple-element.8), kind=kLoop, calls=%fused_computation.1 | loop fusion | flops 65536 | bytes 524288 | tf_op jit(solution)/shard_map/mul | solution.py:671
  34.8 0.1 mul.35
  35.0 0.2 copy.26
  35.2 0.8 %copy.27.mass_ref = f32[256,256]{1,0:T(8,128)} copy(f32[256,256]{0,1:T(8,128)S(1)} %bitcast.23) | data formatting | bytes 524288 | tf_op jit(solution)/shard_map/mul | solution.py:671
  36.0 38.7 %shard_map.194 = f32[4,128,128]{2,1,0:T(8,128)} custom-call(f32[4,128,128]{2,1,0:T(8,128)} %bitcast.21, f32[256,256]{1,0:T(8,128)} %copy.27.mass_ref, bf16[512,256]{1,0:T(8,128)(2,1)} %constant.93.clone.x_high_ref, bf16[512,256]{1,0:T(8,128)(2,1)} %constant.94.clone.x_low_ref, f32[4,1024,512]{2,1,0:T(8,128)} %constant.95.clone.y_ref), custom_call_target="tpu_custom_call" | custom-call | tf_op jit(solution)/shard_map/pallas_call | solution.py:559
  74.7 1.8 %copy.28 = f32[1,128,4,128]{3,2,1,0:T(4,128)} copy(f32[1,128,4,128]{3,1,2,0:T(8,128)} %bitcast.22) | data formatting | bytes 524288
  76.5 0.0 copy-done.1
  76.5 0.7 copy.33
  77.2 0.0 copy-done
  77.2 0.7 copy.34
  (2 shorter events, 0.0 us)
Async XLA Ops:
  32.1 44.4 %copy-start.1 = (f32[512,128]{1,0:T(8,128)S(1)}, f32[512,128]{1,0:T(8,128)}, u32[]{:S(2)}) copy-start(f32[512,128]{1,0:T(8,128)} %get-tuple-element.9) | copy-start | bytes 786436
  32.1 45.1 %copy-start = (f32[512,128]{1,0:T(8,128)S(1)}, f32[512,128]{1,0:T(8,128)}, u32[]{:S(2)}) copy-start(f32[512,128]{1,0:T(8,128)} %get-tuple-element.10) | copy-start | bytes 786436

commit v3 on v2

--- a/solution.py
+++ b/solution.py
@@ -578,7 +578,7 @@
             pltpu.SemaphoreType.DMA,
         ],
         compiler_params=pltpu.CompilerParams(
-            collective_id=1, has_side_effects=True, vmem_limit_bytes=60 * 2**20
+            collective_id=1, has_side_effects=True, vmem_limit_bytes=57 * 2**20
         ),
     )(grad, mass, *x_tables, jnp.asarray(y_table))
 

time: 78.3 us -> 78.3 us (level)
  no operation moved by 1% of the time
where the time goes in v3:
time: 78.3 us; the launch traced here: 78 us
  Pallas kernels  66.4 us (85%)
  local copies, waits for them, and re-layouts  7.85 us (10%)
  other arithmetic  3.01 us (4%)
    pallas_call x1, Pallas kernels, run_spectral(): pl.pallas_call(spectral_kernel, out_shape=jax.ShapeDtypeStruct(grad.shape...  38.7 us
    pallas_call x1, Pallas kernels, run_window(): pl.pallas_call(functools.partial(window_kernel, chunk, move_mass), out_sh...  27.7 us
    unnamed x8, local copies, waits for them, and re-layouts  4.17 us
    reshape x1, local copies, waits for them, and re-layouts, per_device(): by_plane = gradient.reshape(x_rows, z_depth, y_cols).transpose(1, 0, 2)  1.73 us

profile of v3, /device:TPU:31, one launch (start us, length us, event | category | flops | bytes accessed | tf_op | source)
XLA Modules:
  0.0 78.0 jit_solution(8254919498598672187)
XLA Ops:
  0.6 0.1 pad.3.clone
  0.7 0.7 convert_bitcast_fusion
  1.4 1.3 %maximum_maximum_fusion.rec_ref = f32[8,128]{1,0:T(8,128)} fusion(f32[4,128]{1,0:T(4,128)} %param.25, f32[1,128]{1,0:T(1,128)S(1)} %fusion.2, f32[1,128]{1,0:T(1,128)S(1)} %get-tuple-element.17, f32[8]{0:T(128)S(1)} %pad.3.clone), kind=kLoop, calls=%fused_computation.2 | loop fusion | flops 3072 | bytes 7200 | tf_op jit(solution)/shard_map/concatenate | solution.py:647
  2.8 0.9 %copy.24 = f32[256,64]{1,0:T(8,128)S(1)} copy(f32[256,64]{0,1:T(8,128)} %param.26) | data formatting | bytes 131072 | tf_op args[8]
  3.7 0.7 reshape.47.mass_ref
  4.4 27.7 %shard_map.193 = (f32[512,128]{1,0:T(8,128)}, f32[512,128]{1,0:T(8,128)}, f32[512,128]{1,0:T(8,128)}, f32[4,128,128]{2,1,0:T(8,128)}) custom-call(f32[512,128]{1,0:T(8,128)} %bitcast.24, f32[512,128]{1,0:T(8,128)} %bitcast.25, f32[512,128]{1,0:T(8,128)} %bitcast.26, f32[512,128]{1,0:T(8,128)} %bitcast.27, f32[512,128]{1,0:T(8,128)} %bitcast.28, ...), custom_call_target="tpu_custom_call" | custom-call | tf_op jit(solution)/shard_map/pallas_call | solution.py:328
  32.1 0.0 copy-start.1
  32.1 0.0 copy-start
  32.1 1.7 %copy.30 = f32[128,4,128]{2,0,1:T(8,128)} copy(f32[128,4,128]{2,1,0:T(4,128)} %bitcast.31) | data formatting | bytes 524288 | tf_op jit(solution)/shard_map/reshape | solution.py:669
  33.9 1.0 %broadcast_multiply_fusion = f32[4,128,128]{2,1,0:T(8,128)S(1)} fusion(f32[4,128,128]{2,1,0:T(8,128)} %get-tuple-element.8), kind=kLoop, calls=%fused_computation.1 | loop fusion | flops 65536 | bytes 524288 | tf_op jit(solution)/shard_map/mul | solution.py:671
  34.8 0.1 mul.35
  35.0 0.2 copy.26
  35.2 0.8 %copy.27.mass_ref = f32[256,256]{1,0:T(8,128)} copy(f32[256,256]{0,1:T(8,128)S(1)} %bitcast.23) | data formatting | bytes 524288 | tf_op jit(solution)/shard_map/mul | solution.py:671
  36.0 38.7 %shard_map.194 = f32[4,128,128]{2,1,0:T(8,128)} custom-call(f32[4,128,128]{2,1,0:T(8,128)} %bitcast.21, f32[256,256]{1,0:T(8,128)} %copy.27.mass_ref, bf16[512,256]{1,0:T(8,128)(2,1)} %constant.93.clone.x_high_ref, bf16[512,256]{1,0:T(8,128)(2,1)} %constant.94.clone.x_low_ref, f32[4,1024,512]{2,1,0:T(8,128)} %constant.95.clone.y_ref), custom_call_target="tpu_custom_call" | custom-call | tf_op jit(solution)/shard_map/pallas_call | solution.py:559
  74.7 1.8 %copy.28 = f32[1,128,4,128]{3,2,1,0:T(4,128)} copy(f32[1,128,4,128]{3,1,2,0:T(8,128)} %bitcast.22) | data formatting | bytes 524288
  76.5 0.0 copy-done.1
  76.5 0.7 copy.33
  77.2 0.0 copy-done
  77.2 0.7 copy.34
  (2 shorter events, 0.0 us)
Async XLA Ops:
  32.1 44.4 %copy-start.1 = (f32[512,128]{1,0:T(8,128)S(1)}, f32[512,128]{1,0:T(8,128)}, u32[]{:S(2)}) copy-start(f32[512,128]{1,0:T(8,128)} %get-tuple-element.9) | copy-start | bytes 786436
  32.1 45.1 %copy-start = (f32[512,128]{1,0:T(8,128)S(1)}, f32[512,128]{1,0:T(8,128)}, u32[]{:S(2)}) copy-start(f32[512,128]{1,0:T(8,128)} %get-tuple-element.10) | copy-start | bytes 786436
